TPU v7x, 32 devices: a whole 2x2x4 slice. The times are simulated.
32 devices in a mesh: blk: 8 (over z, x), win: 4 (over y, core).
Axes of the slice: x: 2, y: 2, z: 4, core: 2. Of those that a mesh axis runs over, the one named last changes fastest.
Arguments:
- samples: bfloat16 [1024, 32, 2048], P('blk', 'win'), may hold values from -6 to 6
- pair_offsets: int32 [24], P('blk'), may hold values from 0 to 4, as said below
- pair_count: int32 [8], P('blk'), may hold values from 1 to 3
Outputs:
- cross_spectra: bfloat16 [24, 128, 2, 128, 128], P('blk', 'win')
Inputs may be any that keep to these rules, and one draw needn't show every extreme that they name: `pair_offsets`: entry w * 3 + s belongs to worker w. The live slots of a worker (s below its count) hold different offsets, with w + offset below the number of blocks; the other slots hold 0.
All inputs are finite; a program needn't handle non-finite values.
Results may differ from a plain program's by a relative error of at most 0.0068.
Values may be sent and summed in bfloat16 or wider, within the bound.
A program may use at most 64 MiB of HBM per device.

v0:
```python
import math
import jax
import jax.numpy as jnp
from jax import lax
from jax.sharding import PartitionSpec as P

BINS = 128
BIN0 = 32
SMOOTH = 4
OFFSET = 4
water_level = 0.1
epsilon = 1e-06


def shifted(block, axis, distance):
    devices = range(lax.axis_size(axis))
    route = [(i - distance, i) for i in devices if i - distance in devices]
    return lax.ppermute(block, axis, route)


def dft_table(length):
    sample_idx = jnp.arange(length, dtype=jnp.int32)
    bin_freqs = BIN0 + jnp.arange(BINS, dtype=jnp.int32)
    phases = sample_idx[:, None] * bin_freqs[None, :] % length
    angles = phases.astype(jnp.float32) * (2.0 * math.pi / length)
    window_taper = 0.5 - 0.5 * jnp.cos(
        (sample_idx.astype(jnp.float32) + 0.5) * (2.0 * math.pi / length)
    )
    cosines = window_taper[:, None] * jnp.cos(angles)
    sines = -window_taper[:, None] * jnp.sin(angles)
    return jnp.concatenate([cosines, sines], axis=1).astype(jnp.bfloat16)


def band_weights():
    bin_index = jnp.arange(BINS, dtype=jnp.int32)
    inside = (jnp.abs(bin_index[:, None] - bin_index[None, :]) <= SMOOTH).astype(jnp.float32)
    return inside / jnp.sum(inside, axis=0, keepdims=True)


def whiten_spectrum(spectrum, weights):
    energy = spectrum[:, 0] * spectrum[:, 0] + spectrum[:, 1] * spectrum[:, 1]
    smoothed = jnp.einsum("wjc,jb->wbc", energy, weights, precision=lax.Precision.HIGHEST)
    average = jnp.mean(energy, axis=1, keepdims=True)
    factor = lax.rsqrt(smoothed + water_level * average + epsilon)
    return (spectrum * factor[:, None]).astype(jnp.bfloat16)


def cross_pair(left_side, partner, windows):
    right_side = partner.reshape(2 * windows, partner.shape[2], partner.shape[3])
    product = lax.dot_general(
        left_side, right_side, (((1,), (0,)), ((2,), (1,))), preferred_element_type=jnp.float32
    )
    return product * (1.0 / windows)


def shards(samples, pair_offsets, pair_count):
    channels, win_dev, length = samples.shape
    table = dft_table(length)
    weights = band_weights()
    spectrum = jnp.einsum("cwt,tk->wkc", samples, table, preferred_element_type=jnp.float32)
    whitened = whiten_spectrum(spectrum.reshape(win_dev, 2, BINS, channels), weights)
    by_bins = lax.all_to_all(whitened, "win", split_axis=2, concat_axis=0, tiled=True)
    windows = by_bins.shape[0]
    bins_dev = by_bins.shape[2]
    swapped = jnp.stack([by_bins[:, 1], -by_bins[:, 0]], axis=1)
    left_side = jnp.stack([by_bins, swapped], axis=0).reshape(2, 2 * windows, bins_dev, channels)
    neighbours = [by_bins]
    for distance in range(1, OFFSET + 1):
        neighbours.append(shifted(by_bins, "blk", -distance))
    nearby = jnp.stack(neighbours, axis=0)
    live_count = pair_count[0]
    slot_total = pair_offsets.shape[0]
    results = []
    for slot_rank in range(slot_total):
        partner = lax.dynamic_index_in_dim(nearby, pair_offsets[slot_rank], 0, keepdims=False)
        value = cross_pair(left_side, partner, windows)
        results.append(
            jnp.where(slot_rank < live_count, value, jnp.zeros_like(value)).astype(jnp.bfloat16)
        )
    cross_spectra = jnp.stack(results, axis=0)
    return cross_spectra


def solution(mesh):
    in_specs = (P("blk", "win", None), P("blk"), P("blk"))
    out_specs = P("blk", "win", None, None, None)
    return jax.shard_map(shards, mesh=mesh, in_specs=in_specs, out_specs=out_specs, check_vma=False)
```

profile of v0, /device:TPU:0, one launch (start us, length us, event | category | flops | bytes accessed | tf_op | source)
XLA Modules:
  0.0 109.8 jit_solution(9315533526000073080)
XLA Ops:
  0.0 0.1 convert_reduce_fusion
  0.1 0.1 multiply_subtract_fusion
  0.2 4.5 %multiply_convert_fusion.2 = (bf16[2048,128]{0,1:T(8,128)(2,1)S(1)}, bf16[2048,128]{0,1:T(8,128)(2,1)S(1)}) fusion(s32[128]{0:T(128)S(1)} %iota_add_fusion, f32[2048]{0:T(1024)S(1)} %get-tuple-element.15, f32[2048]{0:T(1024)S(1)} %get-tuple-element.16), kind=kLoop, calls=%fused_computation.25 | loop fusion | flops 4718592 | bytes 1065472 | tf_op jit(solution)/shard_map/convert
  4.7 7.1 %fusion = f32[256,128,8]{1,0,2:T(8,128)S(1)} fusion(bf16[128,8,2048]{2,1,0:T(8,128)(2,1)} %param.3, bf16[2048,128]{0,1:T(8,128)(2,1)S(1)} %get-tuple-element.14, bf16[2048,128]{0,1:T(8,128)(2,1)S(1)} %get-tuple-element.13), kind=kOutput, calls=%fused_computation.1 | convolution fusion | flops 1075838976 | bytes 6291456 | tf_op jit(solution)/shard_map/cwt,tk->wkc/dot_general | solution.py:60
  11.9 0.1 fusion.18
  12.0 0.0 copy-start
  12.0 0.6 fusion.7
  12.7 0.1 multiply_convert_fusion
  12.8 1.3 %copy.15 = bf16[8,2,128,128]{3,1,0,2:T(2,128)(2,1)} copy(bf16[8,2,128,128]{3,2,1,0:T(8,128)(2,1)S(1)} %multiply_convert_fusion) | data formatting | bytes 1048576 | tf_op jit(solution)/shard_map/convert_element_type | solution.py:45
  14.1 4.2 %all-to-all-start = ((bf16[8,2,128,128]{3,1,0,2:T(2,128)(2,1)}), bf16[8,2,128,128]{3,1,0,2:T(2,128)(2,1)S(1)}, u32[]{:S(2)}, u32[]{:S(2)}) async-start(bf16[8,2,128,128]{3,1,0,2:T(2,128)(2,1)} %copy.15), calls=%async_computation | async-start | bytes 1048576 | tf_op jit(solution)/shard_map/all_to_all | solution.py:62
  18.3 0.0 copy-done
  18.3 0.7 fusion.31
  25.2 1.9 %all-to-all-done = bf16[8,2,128,128]{3,1,0,2:T(2,128)(2,1)S(1)} async-done(((bf16[8,2,128,128]{3,1,0,2:T(2,128)(2,1)}), bf16[8,2,128,128]{3,1,0,2:T(2,128)(2,1)S(1)}, u32[]{:S(2)}, u32[]{:S(2)}) %all-to-all-start) | async-done | bytes 524320 | tf_op jit(solution)/shard_map/all_to_all | solution.py:62
  27.2 0.5 copy.16
  27.7 1.3 %collective-permute-start.2 = (bf16[32,2,32,128]{3,1,0,2:T(2,128)(2,1)S(1)}, bf16[32,2,32,128]{3,1,0,2:T(2,128)(2,1)S(1)}, u32[]{:S(2)}, u32[]{:S(2)}) collective-permute-start(bf16[32,2,32,128]{3,1,0,2:T(2,128)(2,1)S(1)} %bitcast.62), channel_id=1, source_target_pairs={{12,0},{16,4},{20,8},{24,12},{28,16},{13,1},{17,5},{21,9},{25,13},... | collective-permute-start | bytes 1572872 | tf_op jit(solution)/shard_map/ppermute | solution.py:18
  29.0 1.3 %collective-permute-start.1 = (bf16[32,2,32,128]{3,1,0,2:T(2,128)(2,1)S(1)}, bf16[32,2,32,128]{3,1,0,2:T(2,128)(2,1)S(1)}, u32[]{:S(2)}, u32[]{:S(2)}) collective-permute-start(bf16[32,2,32,128]{3,1,0,2:T(2,128)(2,1)S(1)} %bitcast.63), channel_id=1, source_target_pairs={{8,0},{12,4},{16,8},{20,12},{24,16},{28,20},{9,1},{13,5},{17,9},{2... | collective-permute-start | bytes 1572872 | tf_op jit(solution)/shard_map/ppermute | solution.py:18
  30.3 1.3 %collective-permute-start = (bf16[32,2,32,128]{3,1,0,2:T(2,128)(2,1)S(1)}, bf16[32,2,32,128]{3,1,0,2:T(2,128)(2,1)S(1)}, u32[]{:S(2)}, u32[]{:S(2)}) collective-permute-start(bf16[32,2,32,128]{3,1,0,2:T(2,128)(2,1)S(1)} %bitcast.64), channel_id=1, source_target_pairs={{4,0},{8,4},{12,8},{16,12},{20,16},{24,20},{28,24},{5,1},{9,5},{13... | collective-permute-start | bytes 1572872 | tf_op jit(solution)/shard_map/ppermute | solution.py:18
  31.6 1.5 %collective-permute-start.3 = (bf16[32,2,32,128]{3,1,0,2:T(2,128)(2,1)S(1)}, bf16[32,2,32,128]{3,1,0,2:T(2,128)(2,1)S(1)}, u32[]{:S(2)}, u32[]{:S(2)}) collective-permute-start(bf16[32,2,32,128]{3,1,0,2:T(2,128)(2,1)S(1)} %bitcast.65), channel_id=1, source_target_pairs={{16,0},{20,4},{24,8},{28,12},{17,1},{21,5},{25,9},{29,13},{18,2},{... | collective-permute-start | bytes 1572872 | tf_op jit(solution)/shard_map/ppermute | solution.py:18
  33.1 0.9 fusion.30
  34.1 0.4 constant_dynamic-update-slice_fusion
  34.5 1.2 %pad_maximum_fusion.2 = bf16[32,2,32,128]{3,1,0,2:T(2,128)(2,1)S(1)} fusion(bf16[32,1,32,128]{3,1,0,2:T(2,128)(2,1)S(1)} %get-tuple-element.9, bf16[32,1,32,128]{3,1,0,2:T(2,128)(2,1)S(1)} %get-tuple-element.8), kind=kLoop, calls=%fused_computation.33 | loop fusion | flops 1048576 | bytes 1048576 | tf_op jit(solution)/shard_map/stack | solution.py:65
  35.7 20.0 %collective-permute-done = bf16[32,2,32,128]{3,1,0,2:T(2,128)(2,1)S(1)} collective-permute-done((bf16[32,2,32,128]{3,1,0,2:T(2,128)(2,1)S(1)}, bf16[32,2,32,128]{3,1,0,2:T(2,128)(2,1)S(1)}, u32[]{:S(2)}, u32[]{:S(2)}) %collective-permute-start) | collective-permute-done | bytes 524320 | tf_op jit(solution)/shard_map/ppermute | solution.py:18
  55.7 0.5 bitcast_dynamic-update-slice_fusion.3
  56.2 0.0 collective-permute-done.1
  56.3 0.5 bitcast_dynamic-update-slice_fusion.2
  56.8 0.0 collective-permute-done.2
  56.8 0.5 bitcast_dynamic-update-slice_fusion.1
  57.3 44.6 %collective-permute-done.3 = bf16[32,2,32,128]{3,1,0,2:T(2,128)(2,1)S(1)} collective-permute-done((bf16[32,2,32,128]{3,1,0,2:T(2,128)(2,1)S(1)}, bf16[32,2,32,128]{3,1,0,2:T(2,128)(2,1)S(1)}, u32[]{:S(2)}, u32[]{:S(2)}) %collective-permute-start.3) | collective-permute-done | bytes 524320 | tf_op jit(solution)/shard_map/ppermute | solution.py:18
  101.8 0.5 bitcast_dynamic-update-slice_fusion
  102.3 1.5 %constant_dynamic-slice_fusion.2 = (bf16[1,32,2,32,128]{4,2,1,3,0:T(2,128)(2,1)S(1)}, bf16[1,32,2,32,128]{4,2,1,3,0:T(2,128)(2,1)S(1)}, bf16[1,32,2,32,128]{4,2,1,3,0:T(2,128)(2,1)S(1)}) fusion(bf16[5,32,2,32,128]{4,2,1,3,0:T(2,128)(2,1)S(1)} %bitcast_dynamic-update-slice_fusion, s32[]{:T(128)S(6)} %select_n.41, s32[]{:T(128)S(6)} %select_n.47, s32[]{:T(128)S(6)} %select_n.44), kind=kLoop, calls=%fused_computation.52 | loop fusion | bytes 3145740 | tf_op jit(solution)/shard_map/jit(dynamic_index_in_dim)/dynamic_slice | solution.py:75
  103.8 0.9 fusion.4
  104.7 0.9 fusion.2
  105.7 0.9 fusion.3
  106.6 3.2 %pad_maximum_fusion = bf16[3,32,2,128,128]{4,3,2,1,0:T(8,128)(2,1)} fusion(bf16[1,32,2,128,128]{4,3,2,1,0:T(8,128)(2,1)S(1)} %fusion.4, bf16[1,32,2,128,128]{4,3,2,1,0:T(8,128)(2,1)S(1)} %fusion.3, bf16[1,32,2,128,128]{4,3,2,1,0:T(8,128)(2,1)S(1)} %fusion.2), kind=kLoop, calls=%fused_computation | loop fusion | flops 6291456 | bytes 12582912 | tf_op jit(solution)/shard_map/stack | solution.py:80
  (2 shorter events, 0.0 us)
Async XLA Ops:
  12.0 6.4 %copy-start = (s32[3]{0:T(128)S(1)}, s32[3]{0:T(128)}, u32[]{:S(2)}) copy-start(s32[3]{0:T(128)} %param.4) | copy-start | bytes 40
  14.1 13.1 %all-to-all-start = ((bf16[8,2,128,128]{3,1,0,2:T(2,128)(2,1)}), bf16[8,2,128,128]{3,1,0,2:T(2,128)(2,1)S(1)}, u32[]{:S(2)}, u32[]{:S(2)}) async-start(bf16[8,2,128,128]{3,1,0,2:T(2,128)(2,1)} %copy.15), calls=%async_computation | async-start | bytes 1048576 | tf_op jit(solution)/shard_map/all_to_all | solution.py:62
  27.7 29.0 %collective-permute-start.2 = (bf16[32,2,32,128]{3,1,0,2:T(2,128)(2,1)S(1)}, bf16[32,2,32,128]{3,1,0,2:T(2,128)(2,1)S(1)}, u32[]{:S(2)}, u32[]{:S(2)}) collective-permute-start(bf16[32,2,32,128]{3,1,0,2:T(2,128)(2,1)S(1)} %bitcast.62), channel_id=1, source_target_pairs={{12,0},{16,4},{20,8},{24,12},{28,16},{13,1},{17,5},{21,9},{25,13},... | collective-permute-start | bytes 1572872 | tf_op jit(solution)/shard_map/ppermute | solution.py:18
  29.0 27.2 %collective-permute-start.1 = (bf16[32,2,32,128]{3,1,0,2:T(2,128)(2,1)S(1)}, bf16[32,2,32,128]{3,1,0,2:T(2,128)(2,1)S(1)}, u32[]{:S(2)}, u32[]{:S(2)}) collective-permute-start(bf16[32,2,32,128]{3,1,0,2:T(2,128)(2,1)S(1)} %bitcast.63), channel_id=1, source_target_pairs={{8,0},{12,4},{16,8},{20,12},{24,16},{28,20},{9,1},{13,5},{17,9},{2... | collective-permute-start | bytes 1572872 | tf_op jit(solution)/shard_map/ppermute | solution.py:18
  30.3 25.4 %collective-permute-start = (bf16[32,2,32,128]{3,1,0,2:T(2,128)(2,1)S(1)}, bf16[32,2,32,128]{3,1,0,2:T(2,128)(2,1)S(1)}, u32[]{:S(2)}, u32[]{:S(2)}) collective-permute-start(bf16[32,2,32,128]{3,1,0,2:T(2,128)(2,1)S(1)} %bitcast.64), channel_id=1, source_target_pairs={{4,0},{8,4},{12,8},{16,12},{20,16},{24,20},{28,24},{5,1},{9,5},{13... | collective-permute-start | bytes 1572872 | tf_op jit(solution)/shard_map/ppermute | solution.py:18
  31.6 70.2 %collective-permute-start.3 = (bf16[32,2,32,128]{3,1,0,2:T(2,128)(2,1)S(1)}, bf16[32,2,32,128]{3,1,0,2:T(2,128)(2,1)S(1)}, u32[]{:S(2)}, u32[]{:S(2)}) collective-permute-start(bf16[32,2,32,128]{3,1,0,2:T(2,128)(2,1)S(1)} %bitcast.65), channel_id=1, source_target_pairs={{16,0},{20,4},{24,8},{28,12},{17,1},{21,5},{25,9},{29,13},{18,2},{... | collective-permute-start | bytes 1572872 | tf_op jit(solution)/shard_map/ppermute | solution.py:18
where the time goes:
time: 110 us
  waiting for transfers between devices  66.6 us (61%)
  matrix products  10.6 us (10%)
  other arithmetic  10.2 us (9%)
  starting transfers between devices  9.58 us (9%)
  between operations  6.46 us (6%)
  local copies, waits for them, and re-layouts  6.39 us (6%)
    ppermute x4, waiting for transfers between devices, shifted(): return lax.ppermute(block, axis, route)  64.6 us
    dot_general x1, matrix products, shards(): jnp.einsum('cwt,tk->wkc', samples, table, preferred_element_type=jnp.floa...  7.15 us
    ppermute x4, starting transfers between devices, shifted(): return lax.ppermute(block, axis, route)  5.35 us
    another operation x1, other arithmetic  4.53 us
    all_to_all x1, starting transfers between devices, shards(): lax.all_to_all(whitened, 'win', split_axis=2, concat_axis=0, tiled=True)  4.24 us
    another operation x1, other arithmetic, shards(): cross_spectra = jnp.stack(results, axis=0)  3.15 us
    dot_general x3, matrix products, cross_pair(): lax.dot_general(left_side, right_side, (((1,), (0,)), ((2,), (1,))), pref...  2.8 us
  transfers between devices with their start and end apart: 5, of which 3 were waited for; matrix products, arithmetic and copies ran while one was open for 4% of the time, Pallas kernels for 0%

commit v1 on v0

--- a/solution.py
+++ b/solution.py
@@ -10,6 +10,20 @@
 OFFSET = 4
 water_level = 0.1
 epsilon = 1e-06
+
+
+def reach_row_on(xin, axis_k, inputs):
+    later, prior = (xin.shape[:axis_k], xin.shape[axis_k + 1 :])
+    placed = xin.reshape(*later, inputs, -1, *prior)
+    outcome_arr = jnp.moveaxis(placed, axis_k, 0)
+    return outcome_arr
+
+
+def view_leaf(body, array_axis):
+    last = list(body.shape[1:])
+    last[array_axis] *= body.shape[0]
+    arr_now = jnp.moveaxis(body, 0, array_axis).reshape(last)
+    return arr_now
 
 
 def shifted(block, axis, distance):
@@ -59,7 +73,17 @@
     weights = band_weights()
     spectrum = jnp.einsum("cwt,tk->wkc", samples, table, preferred_element_type=jnp.float32)
     whitened = whiten_spectrum(spectrum.reshape(win_dev, 2, BINS, channels), weights)
-    by_bins = lax.all_to_all(whitened, "win", split_axis=2, concat_axis=0, tiled=True)
+    z1 = lax.psum(1, "win")
+    carry_out = lax.axis_index("win")
+    response, right_arr = (z1, carry_out)
+    small = reach_row_on(whitened, 2, response)
+    inbox = [small[right_arr]]
+    for no in range(1, response):
+        y = small[right_arr ^ no]
+        inbox.append(lax.ppermute(y, "win", [(dev, dev ^ no) for dev in range(response)]))
+    m_next = jnp.stack(inbox)
+    small = m_next[right_arr ^ jnp.arange(response)]
+    by_bins = view_leaf(small, 0)
     windows = by_bins.shape[0]
     bins_dev = by_bins.shape[2]
     swapped = jnp.stack([by_bins[:, 1], -by_bins[:, 0]], axis=1)

time: 110 us -> 106 us (0.964)
  waiting for transfers between devices: 66.6 us -> 63.2 us
    all_to_all x1 -> x0, starting transfers between devices: 4.24 us -> none  [shards(): lax.all_to_all(whitened, 'win', split_axis=2, concat_axis=0, tiled=True)]
    ppermute x0 -> x3, starting transfers between devices: none -> 3.15 us  [shards(): lax.ppermute(y, 'win', [(dev, dev ^ no) for dev in range(response)])]
    all_to_all x1 -> x0, waiting for transfers between devices: 1.94 us -> none  [shards(): lax.all_to_all(whitened, 'win', split_axis=2, concat_axis=0, tiled=True)]
    ppermute x4, waiting for transfers between devices: 64.6 us -> 63.2 us  [shifted(): return lax.ppermute(block, axis, route)]
    convert_element_type x1 -> x0, local copies, waits for them, and re-layouts: 1.33 us -> none  [whiten_spectrum(): return (spectrum * factor[:, None]).astype(jnp.bfloat16)]
    gather x0 -> x2, local copies, waits for them, and re-layouts: none -> 1.2 us  [shards(): small = m_next[right_arr ^ jnp.arange(response)]]
    another operation x1 -> x2, other arithmetic: 4.53 us -> 4.6 us
  transfers between devices with their start and end apart: 5 -> 7, of which waited for: 3 -> 2; matrix products, arithmetic and copies ran while one was open for 4% -> 5% of each run, Pallas kernels for 0% -> 0%
where the time goes in v1:
time: 106 us
  waiting for transfers between devices  63.2 us (60%)
  matrix products  10.6 us (10%)
  other arithmetic  10.4 us (10%)
  starting transfers between devices  8.5 us (8%)
  local copies, waits for them, and re-layouts  6.77 us (6%)
  between operations  6.66 us (6%)
    ppermute x4, waiting for transfers between devices, shifted(): return lax.ppermute(block, axis, route)  63.2 us
    dot_general x1, matrix products, shards(): jnp.einsum('cwt,tk->wkc', samples, table, preferred_element_type=jnp.floa...  7.16 us
    ppermute x4, starting transfers between devices, shifted(): return lax.ppermute(block, axis, route)  5.35 us
    another operation x1, other arithmetic  4.53 us
    another operation x1, other arithmetic, shards(): cross_spectra = jnp.stack(results, axis=0)  3.15 us
    ppermute x3, starting transfers between devices, shards(): lax.ppermute(y, 'win', [(dev, dev ^ no) for dev in range(response)])  3.15 us
    dot_general x3, matrix products, cross_pair(): lax.dot_general(left_side, right_side, (((1,), (0,)), ((2,), (1,))), pref...  2.78 us
  transfers between devices with their start and end apart: 7, of which 2 were waited for; matrix products, arithmetic and copies ran while one was open for 5% of the time, Pallas kernels for 0%

profile of v1, /device:TPU:0, one launch (start us, length us, event | category | flops | bytes accessed | tf_op | source)
XLA Modules:
  0.0 106.1 jit_solution(10812640852230758182)
XLA Ops:
  0.0 0.1 convert_reduce_fusion
  0.1 0.1 multiply_subtract_fusion
  0.2 4.5 %multiply_convert_fusion.2 = (bf16[2048,128]{0,1:T(8,128)(2,1)S(1)}, bf16[2048,128]{0,1:T(8,128)(2,1)S(1)}) fusion(s32[128]{0:T(128)S(1)} %iota_add_fusion, f32[2048]{0:T(1024)S(1)} %get-tuple-element.19, f32[2048]{0:T(1024)S(1)} %get-tuple-element.20), kind=kLoop, calls=%fused_computation.25 | loop fusion | flops 4718592 | bytes 1065472 | tf_op jit(solution)/shard_map/convert
  4.7 7.2 %fusion = f32[256,128,8]{1,0,2:T(8,128)S(1)} fusion(bf16[128,8,2048]{2,1,0:T(8,128)(2,1)} %param.3, bf16[2048,128]{0,1:T(8,128)(2,1)S(1)} %get-tuple-element.18, bf16[2048,128]{0,1:T(8,128)(2,1)S(1)} %get-tuple-element.17), kind=kOutput, calls=%fused_computation.2 | convolution fusion | flops 1075838976 | bytes 6291456 | tf_op jit(solution)/shard_map/cwt,tk->wkc/dot_general | solution.py:74
  11.9 0.0 copy-start
  11.9 0.1 fusion.19
  12.0 0.6 fusion.6
  12.7 0.2 multiply_convert_fusion
  12.9 2.5 %collective-permute-start.2 = (bf16[8,2,32,128]{3,2,1,0:T(8,128)(2,1)S(1)}, bf16[8,2,32,128]{3,2,1,0:T(8,128)(2,1)S(1)}, u32[]{:S(2)}, u32[]{:S(2)}) collective-permute-start(bf16[8,2,32,128]{3,2,1,0:T(8,128)(2,1)S(1)} %get-tuple-element.11), channel_id=1, source_target_pairs={{0,3},{1,2},{2,1},{3,0},{4,7},{5,6},{6,5},{7,4},{8,11},{9,10},{10,... | collective-permute-start | bytes 393224 | tf_op jit(solution)/shard_map/ppermute | solution.py:83
  15.4 0.6 collective-permute-start.1
  16.0 0.0 collective-permute-start
  16.1 0.0 copy-done
  16.1 0.6 fusion.33
  23.1 0.0 collective-permute-done.2
  23.1 0.0 collective-permute-done.1
  23.1 0.0 collective-permute-done
  23.1 0.1 pad_maximum_fusion.2
  23.2 0.6 gather_fusion
  23.9 0.5 copy.11
  24.4 1.3 %collective-permute-start.4 = (bf16[32,2,32,128]{3,1,0,2:T(2,128)(2,1)S(1)}, bf16[32,2,32,128]{3,1,0,2:T(2,128)(2,1)S(1)}, u32[]{:S(2)}, u32[]{:S(2)}) collective-permute-start(bf16[32,2,32,128]{3,1,0,2:T(2,128)(2,1)S(1)} %copy.11), channel_id=1, source_target_pairs={{8,0},{12,4},{16,8},{20,12},{24,16},{28,20},{9,1},{13,5},{17,9},{2... | collective-permute-start | bytes 1572872 | tf_op jit(solution)/shard_map/ppermute | solution.py:32
  25.7 1.3 %collective-permute-start.3 = (bf16[32,2,32,128]{3,1,0,2:T(2,128)(2,1)S(1)}, bf16[32,2,32,128]{3,1,0,2:T(2,128)(2,1)S(1)}, u32[]{:S(2)}, u32[]{:S(2)}) collective-permute-start(bf16[32,2,32,128]{3,1,0,2:T(2,128)(2,1)S(1)} %copy.11), channel_id=1, source_target_pairs={{4,0},{8,4},{12,8},{16,12},{20,16},{24,20},{28,24},{5,1},{9,5},{13... | collective-permute-start | bytes 1572872 | tf_op jit(solution)/shard_map/ppermute | solution.py:32
  27.0 0.9 fusion.32
  28.0 1.2 %pad_maximum_fusion.3 = bf16[32,2,32,128]{3,1,0,2:T(2,128)(2,1)S(1)} fusion(bf16[32,1,32,128]{3,1,0,2:T(2,128)(2,1)S(1)} %get-tuple-element.9, bf16[32,1,32,128]{3,1,0,2:T(2,128)(2,1)S(1)} %get-tuple-element.8), kind=kLoop, calls=%fused_computation.36 | loop fusion | flops 1048576 | bytes 1048576 | tf_op jit(solution)/shard_map/stack | solution.py:89
  29.2 0.5 copy.10
  29.7 1.3 %collective-permute-start.5 = (bf16[32,2,32,128]{3,1,0,2:T(2,128)(2,1)S(1)}, bf16[32,2,32,128]{3,1,0,2:T(2,128)(2,1)S(1)}, u32[]{:S(2)}, u32[]{:S(2)}) collective-permute-start(bf16[32,2,32,128]{3,1,0,2:T(2,128)(2,1)S(1)} %copy.11), channel_id=1, source_target_pairs={{12,0},{16,4},{20,8},{24,12},{28,16},{13,1},{17,5},{21,9},{25,13},... | collective-permute-start | bytes 1572872 | tf_op jit(solution)/shard_map/ppermute | solution.py:32
  31.0 1.5 %collective-permute-start.6 = (bf16[32,2,32,128]{3,1,0,2:T(2,128)(2,1)S(1)}, bf16[32,2,32,128]{3,1,0,2:T(2,128)(2,1)S(1)}, u32[]{:S(2)}, u32[]{:S(2)}) collective-permute-start(bf16[32,2,32,128]{3,1,0,2:T(2,128)(2,1)S(1)} %copy.11), channel_id=1, source_target_pairs={{16,0},{20,4},{24,8},{28,12},{17,1},{21,5},{25,9},{29,13},{18,2},{... | collective-permute-start | bytes 1572872 | tf_op jit(solution)/shard_map/ppermute | solution.py:32
  32.5 0.5 copy_dynamic-update-slice_fusion
  33.1 20.1 %collective-permute-done.3 = bf16[32,2,32,128]{3,1,0,2:T(2,128)(2,1)S(1)} collective-permute-done((bf16[32,2,32,128]{3,1,0,2:T(2,128)(2,1)S(1)}, bf16[32,2,32,128]{3,1,0,2:T(2,128)(2,1)S(1)}, u32[]{:S(2)}, u32[]{:S(2)}) %collective-permute-start.3) | collective-permute-done | bytes 524320 | tf_op jit(solution)/shard_map/ppermute | solution.py:32
  53.2 0.5 bitcast_dynamic-update-slice_fusion.3
  53.7 0.0 collective-permute-done.4
  53.7 0.5 bitcast_dynamic-update-slice_fusion.2
  54.2 0.0 collective-permute-done.5
  54.2 0.5 bitcast_dynamic-update-slice_fusion.1
  54.7 43.1 %collective-permute-done.6 = bf16[32,2,32,128]{3,1,0,2:T(2,128)(2,1)S(1)} collective-permute-done((bf16[32,2,32,128]{3,1,0,2:T(2,128)(2,1)S(1)}, bf16[32,2,32,128]{3,1,0,2:T(2,128)(2,1)S(1)}, u32[]{:S(2)}, u32[]{:S(2)}) %collective-permute-start.6) | collective-permute-done | bytes 524320 | tf_op jit(solution)/shard_map/ppermute | solution.py:32
  97.8 0.5 bitcast_dynamic-update-slice_fusion
  98.3 1.8 %constant_dynamic-slice_fusion.2 = (bf16[1,32,2,32,128]{4,2,1,3,0:T(2,128)(2,1)S(1)}, bf16[1,32,2,32,128]{4,2,1,3,0:T(2,128)(2,1)S(1)}, bf16[1,32,2,32,128]{4,2,1,3,0:T(2,128)(2,1)S(1)}) fusion(bf16[5,32,2,32,128]{4,2,1,3,0:T(2,128)(2,1)S(1)} %bitcast_dynamic-update-slice_fusion, s32[]{:T(128)S(6)} %select_n.68, s32[]{:T(128)S(6)} %select_n.74, s32[]{:T(128)S(6)} %select_n.71), kind=kLoop, calls=%fused_computation.61 | loop fusion | bytes 3145740 | tf_op jit(solution)/shard_map/jit(dynamic_index_in_dim)/dynamic_slice | solution.py:99
  100.1 0.9 fusion.4
  101.1 0.9 fusion.2
  102.0 0.9 fusion.3
  103.0 3.2 %pad_maximum_fusion = bf16[3,32,2,128,128]{4,3,2,1,0:T(8,128)(2,1)} fusion(bf16[1,32,2,128,128]{4,3,2,1,0:T(8,128)(2,1)S(1)} %fusion.4, bf16[1,32,2,128,128]{4,3,2,1,0:T(8,128)(2,1)S(1)} %fusion.3, bf16[1,32,2,128,128]{4,3,2,1,0:T(8,128)(2,1)S(1)} %fusion.2), kind=kLoop, calls=%fused_computation.1 | loop fusion | flops 6291456 | bytes 12582912 | tf_op jit(solution)/shard_map/stack | solution.py:104
  (5 shorter events, 0.1 us)
Async XLA Ops:
  11.9 4.2 %copy-start = (s32[3]{0:T(128)S(1)}, s32[3]{0:T(128)}, u32[]{:S(2)}) copy-start(s32[3]{0:T(128)} %param.4) | copy-start | bytes 40
  12.9 10.2 %collective-permute-start.2 = (bf16[8,2,32,128]{3,2,1,0:T(8,128)(2,1)S(1)}, bf16[8,2,32,128]{3,2,1,0:T(8,128)(2,1)S(1)}, u32[]{:S(2)}, u32[]{:S(2)}) collective-permute-start(bf16[8,2,32,128]{3,2,1,0:T(8,128)(2,1)S(1)} %get-tuple-element.11), channel_id=1, source_target_pairs={{0,3},{1,2},{2,1},{3,0},{4,7},{5,6},{6,5},{7,4},{8,11},{9,10},{10,... | collective-permute-start | bytes 393224 | tf_op jit(solution)/shard_map/ppermute | solution.py:83
  15.4 7.7 %collective-permute-start.1 = (bf16[8,2,32,128]{3,2,1,0:T(8,128)(2,1)S(1)}, bf16[8,2,32,128]{3,2,1,0:T(8,128)(2,1)S(1)}, u32[]{:S(2)}, u32[]{:S(2)}) collective-permute-start(bf16[8,2,32,128]{3,2,1,0:T(8,128)(2,1)S(1)} %get-tuple-element.12), channel_id=1, source_target_pairs={{0,2},{1,3},{2,0},{3,1},{4,6},{5,7},{6,4},{7,5},{8,10},{9,11},{10,... | collective-permute-start | bytes 393224 | tf_op jit(solution)/shard_map/ppermute | solution.py:83
  16.0 7.1 %collective-permute-start = (bf16[8,2,32,128]{3,2,1,0:T(8,128)(2,1)S(1)}, bf16[8,2,32,128]{3,2,1,0:T(8,128)(2,1)S(1)}, u32[]{:S(2)}, u32[]{:S(2)}) collective-permute-start(bf16[8,2,32,128]{3,2,1,0:T(8,128)(2,1)S(1)} %get-tuple-element.13), channel_id=1, source_target_pairs={{0,1},{1,0},{2,3},{3,2},{4,5},{5,4},{6,7},{7,6},{8,9},{9,8},{10,11... | collective-permute-start | bytes 393224 | tf_op jit(solution)/shard_map/ppermute | solution.py:83
  24.4 29.2 %collective-permute-start.4 = (bf16[32,2,32,128]{3,1,0,2:T(2,128)(2,1)S(1)}, bf16[32,2,32,128]{3,1,0,2:T(2,128)(2,1)S(1)}, u32[]{:S(2)}, u32[]{:S(2)}) collective-permute-start(bf16[32,2,32,128]{3,1,0,2:T(2,128)(2,1)S(1)} %copy.11), channel_id=1, source_target_pairs={{8,0},{12,4},{16,8},{20,12},{24,16},{28,20},{9,1},{13,5},{17,9},{2... | collective-permute-start | bytes 1572872 | tf_op jit(solution)/shard_map/ppermute | solution.py:32
  25.7 27.4 %collective-permute-start.3 = (bf16[32,2,32,128]{3,1,0,2:T(2,128)(2,1)S(1)}, bf16[32,2,32,128]{3,1,0,2:T(2,128)(2,1)S(1)}, u32[]{:S(2)}, u32[]{:S(2)}) collective-permute-start(bf16[32,2,32,128]{3,1,0,2:T(2,128)(2,1)S(1)} %copy.11), channel_id=1, source_target_pairs={{4,0},{8,4},{12,8},{16,12},{20,16},{24,20},{28,24},{5,1},{9,5},{13... | collective-permute-start | bytes 1572872 | tf_op jit(solution)/shard_map/ppermute | solution.py:32
  29.7 24.4 %collective-permute-start.5 = (bf16[32,2,32,128]{3,1,0,2:T(2,128)(2,1)S(1)}, bf16[32,2,32,128]{3,1,0,2:T(2,128)(2,1)S(1)}, u32[]{:S(2)}, u32[]{:S(2)}) collective-permute-start(bf16[32,2,32,128]{3,1,0,2:T(2,128)(2,1)S(1)} %copy.11), channel_id=1, source_target_pairs={{12,0},{16,4},{20,8},{24,12},{28,16},{13,1},{17,5},{21,9},{25,13},... | collective-permute-start | bytes 1572872 | tf_op jit(solution)/shard_map/ppermute | solution.py:32
  31.0 66.8 %collective-permute-start.6 = (bf16[32,2,32,128]{3,1,0,2:T(2,128)(2,1)S(1)}, bf16[32,2,32,128]{3,1,0,2:T(2,128)(2,1)S(1)}, u32[]{:S(2)}, u32[]{:S(2)}) collective-permute-start(bf16[32,2,32,128]{3,1,0,2:T(2,128)(2,1)S(1)} %copy.11), channel_id=1, source_target_pairs={{16,0},{20,4},{24,8},{28,12},{17,1},{21,5},{25,9},{29,13},{18,2},{... | collective-permute-start | bytes 1572872 | tf_op jit(solution)/shard_map/ppermute | solution.py:32
